TPU v7x, 32 devices: a whole 2x2x4 slice. The times are simulated.
32 devices in a mesh: rep: 2 (over x), cols: 8 (over z, y), blk: 2 (over core).
Axes of the slice: x: 2, y: 2, z: 4, core: 2. Of those that a mesh axis runs over, the one named last changes fastest.
Arguments:
- acts: bfloat16 [4096, 3584], P(('rep', 'blk'), 'cols'), parts along dimension 0, may hold values from -6 to 6
- grads: bfloat16 [4096, 14336], P(('rep', 'blk'), 'cols'), parts along dimension 0, may hold values from -6 to 6
- eigvecs: bfloat16 [4, 3584, 14336], P('blk', None, 'cols'), may hold values from -0.0008544922 to 0.0008544922
- seg_ids: int32 [4096], P(('rep', 'blk')), parts along dimension 0, may hold values from 0 to 15, never falling along the last dimension, each value on 1 to 256 neighbouring positions
- keep: int32 [4096], P(('rep', 'blk')), parts along dimension 0, may hold values 0 or 1
- queries: float32 [32, 4], P('rep'), parts along dimension 0, may hold values from -6 to 6
- eigvals: float32 [4], replicated, may hold values from 0.25 to 4
Outputs:
- scores: float32 [4, 32], P(None, 'rep'), parts along dimension 1
- influence: float32 [16, 32], P(None, 'rep'), parts along dimension 1
There are 2 independent parts, one for each index of `rep`. A program takes and returns all parts, laid end to end along the dimension named above; an argument that names none is the same for every part. Nothing has to cross between parts.
Inputs may be any that keep to these rules, and one draw needn't show every extreme that they name: `seg_ids`: segment numbers never fall along the tokens; each sequence has 1 to 256 tokens.
All inputs are finite; a program needn't handle non-finite values. No bound on the sum of `keep` on one device may be relied on, other than what follows from the above.
Results may differ from a plain program's by a relative error of at most 0.0003.
Values may be sent and summed in bfloat16 or wider, within the bound.
A program may use at most 192 MiB of HBM per device.

v0:
```python
import math

import jax
import jax.numpy as jnp
from jax import lax
from jax.sharding import PartitionSpec as P

NSEG = 16


def from_behind(block, axis, distance):
    devices = range(lax.axis_size(axis))
    route = [((i - distance) % len(devices), i) for i in devices]
    return lax.ppermute(block, axis, route)


def block_scores(features, grad_rows, weights, seg_rows, keep_rows, nseg):
    proj = jnp.einsum("td,kdf->ktf", features, weights, preferred_element_type=jnp.float32)
    terms = jnp.sum(proj * grad_rows.astype(jnp.float32)[None, :, :], axis=2)
    member = (
        (seg_rows[:, None] == jnp.arange(nseg, dtype=jnp.int32)[None, :])
        & (keep_rows[:, None] == 1)
    ).astype(jnp.float32)
    return jnp.dot(terms, member, precision=lax.Precision.HIGHEST)


def local(acts, grads, eigvecs, seg_ids, keep, queries, eigvals):
    nseg = NSEG
    per_block = eigvecs.shape[0]
    steps = lax.axis_size("blk")
    own_index = lax.axis_index("blk")
    seg_most = acts.shape[0] * steps // 8
    total = jnp.zeros((per_block * steps, nseg), jnp.float32)
    features = lax.all_gather(acts, "cols", axis=1, tiled=True)
    blocks = eigvecs
    for turn in range(steps):
        partial_sums = block_scores(features, grads, blocks, seg_ids, keep, nseg)
        owner = (own_index - turn) % steps
        total = lax.dynamic_update_slice(total, partial_sums, (owner * per_block, jnp.int32(0)))
        if turn + 1 < steps:
            blocks = from_behind(blocks, "blk", 1)
    sums = lax.psum(total, ("cols", "blk"))
    scores = sums * jnp.float32(1.0 / math.sqrt(seg_most))
    weighted = queries / eigvals[None, :]
    influence = jnp.dot(weighted, scores, precision=lax.Precision.HIGHEST)
    return (scores, influence)


def solution(mesh):
    placed = (
        P(("rep", "blk"), "cols"),
        P(("rep", "blk"), "cols"),
        P("blk", None, "cols"),
        P(("rep", "blk")),
        P(("rep", "blk")),
        P("rep", None),
        P(),
    )
    return jax.shard_map(
        local,
        mesh=mesh,
        in_specs=placed,
        out_specs=(P(None, "rep"), P(None, "rep")),
        check_vma=False,
    )
```

profile of v0, /device:TPU:0, one launch (start us, length us, event | category | flops | bytes accessed | tf_op | source)
XLA Modules:
  0.0 228.3 jit_solution(6243914286165730599)
XLA Ops:
  7.2 0.0 all-gather.2.cloned.1.call-start
  7.2 0.5 collective-permute-start
  7.7 0.2 all-gather.2.cloned.1.call-update
  7.9 6.2 %copy.10 = f32[1024,1792]{0,1:T(8,128)} copy(bf16[1024,1792]{1,0:T(8,128)(2,1)} %param.8) | data formatting | bytes 11010048 | tf_op jit(solution)/shard_map/convert_element_type | solution.py:19
  14.1 0.7 broadcast_compare_fusion
  14.8 0.0 copy-start.3
  14.8 110.1 %all-gather.2.cloned.1.call-done = bf16[1024,3584]{0,1:T(8,128)(2,1)} async-done(((bf16[1024,448]{0,1:T(8,128)(2,1)}), bf16[1024,3584]{0,1:T(8,128)(2,1)}) %all-gather.2.cloned.1.call-update) | async-done | bytes 7340048 | tf_op jit(solution)/shard_map/all_gather | solution.py:34
  124.9 0.0 copy-start
  124.9 0.0 copy-start.2
  124.9 32.6 %fusion.1 = f32[2,1024]{1,0:T(2,128)S(1)} fusion(f32[1024,1792]{0,1:T(8,128)} %copy.10, bf16[2,3584,1792]{2,1,0:T(8,128)(2,1)} %param.9, bf16[1024,3584]{0,1:T(8,128)(2,1)} %all-gather.2.cloned.1.call-done), kind=kOutput, calls=%fused_computation.3 | convolution fusion | flops 26314012672 | bytes 40378368 | tf_op jit(solution)/shard_map/td,kdf->ktf/dot_general | solution.py:18
  157.6 0.0 copy-done.3
  157.6 0.5 convolution_dynamic-update-slice_fusion.1
  158.1 0.0 copy-start.4
  158.1 0.0 copy-start.5
  158.1 0.0 collective-permute-done
  158.1 0.0 copy-done
  158.1 0.0 copy-done.2
  158.2 31.4 %fusion = f32[2,1024]{1,0:T(2,128)S(1)} fusion(f32[1024,1792]{0,1:T(8,128)S(1)} %copy-done, bf16[2,3584,1792]{2,1,0:T(8,128)(2,1)} %collective-permute-done, bf16[1024,3584]{0,1:T(8,128)(2,1)S(1)} %copy-done.2), kind=kOutput, calls=%fused_computation.1 | convolution fusion | flops 26314012672 | bytes 40378368 | tf_op jit(solution)/shard_map/td,kdf->ktf/dot_general | solution.py:18
  189.6 0.5 convolution_dynamic-update-slice_fusion
  190.1 30.4 %psum.7 = f32[4,16]{1,0:T(4,128)S(1)} all-reduce(f32[4,16]{1,0:T(4,128)S(1)} %convolution_dynamic-update-slice_fusion), channel_id=1, replica_groups=mesh['rep'=2,'cols'=8,'blk'=2] {'cols','blk'}, use_global_device_ids=true, to_apply=%region_2.3 | all-reduce | flops 64 | bytes 512 | tf_op jit(solution)/shard_map/psum | solution.py:42
  220.5 0.0 copy-done.4
  220.5 0.0 copy-done.5
  220.5 0.0 copy-start.1
  220.5 0.9 fusion.17
  221.4 0.0 copy-done.1
  (2 shorter events, 0.0 us)
Async XLA Ops:
  7.2 117.8 %all-gather.2.cloned.1.call-start = ((), (), s32[]{:S(2)}) async-start(), calls=%async_computation | async-start | bytes 8257536 | tf_op jit(solution)/shard_map/all_gather | solution.py:34
  7.2 150.9 %collective-permute-start = (bf16[2,3584,1792]{2,1,0:T(8,128)(2,1)}, bf16[2,3584,1792]{2,1,0:T(8,128)(2,1)}, u32[]{:S(2)}, u32[]{:S(2)}) collective-permute-start(bf16[2,3584,1792]{2,1,0:T(8,128)(2,1)} %param.9), channel_id=1, source_target_pairs={{1,0},{0,1},{3,2},{2,3},{5,4},{4,5},{7,6},{6,7},{9,8},{8,9},{11,10... | collective-permute-start | bytes 77070344 | tf_op jit(solution)/shard_map/ppermute | solution.py:14
  14.8 142.8 %copy-start.3 = (s32[1024]{0:T(1024)S(1)}, s32[1024]{0:T(1024)}, u32[]{:S(2)}) copy-start(s32[1024]{0:T(1024)} %param.10) | copy-start | bytes 12292
  124.9 33.2 %copy-start = (f32[1024,1792]{0,1:T(8,128)S(1)}, f32[1024,1792]{0,1:T(8,128)}, u32[]{:S(2)}) copy-start(f32[1024,1792]{0,1:T(8,128)} %copy.10) | copy-start | bytes 22020100
  124.9 33.2 %copy-start.2 = (bf16[1024,3584]{0,1:T(8,128)(2,1)S(1)}, bf16[1024,3584]{0,1:T(8,128)(2,1)}, u32[]{:S(2)}) copy-start(bf16[1024,3584]{0,1:T(8,128)(2,1)} %all-gather.2.cloned.1.call-done) | copy-start | bytes 22020100
  158.1 62.4 %copy-start.4 = (f32[16,4]{0,1:T(4,128)S(1)}, f32[16,4]{0,1:T(4,128)}, u32[]{:S(2)}) copy-start(f32[16,4]{0,1:T(4,128)} %param.12) | copy-start | bytes 772
  158.1 62.4 %copy-start.5 = (f32[4]{0:T(128)S(1)}, f32[4]{0:T(128)}, u32[]{:S(2)}) copy-start(f32[4]{0:T(128)} %param.13) | copy-start | bytes 52
  220.5 0.9 copy-start.1
Sparse Core Ops, SparseCore 0:
  10.2 114.6 all-gather.1
where the time goes:
time: 229 us; the launch traced here: 228 us
  waiting for transfers between devices  110 us (48%)
  matrix products  65.9 us (29%)
  blocking collectives  30.4 us (13%)
  between operations  14.1 us (6%)
  local copies, waits for them, and re-layouts  6.23 us (3%)
    all_gather x1, waiting for transfers between devices, local(): features = lax.all_gather(acts, 'cols', axis=1, tiled=True)  110 us
    dot_general x2, matrix products, block_scores(): jnp.einsum('td,kdf->ktf', features, weights, preferred_element_type=jnp.f...  64 us
    psum x1, blocking collectives, local(): sums = lax.psum(total, ('cols', 'blk'))  30.4 us
    convert_element_type x1, local copies, waits for them, and re-layouts, block_scores(): terms = jnp.sum(proj * grad_rows.astype(jnp.float32)[None, :, :], axis=2)  6.2 us
  transfers between devices with their start and end apart: 2, of which 1 were waited for; matrix products, arithmetic and copies ran while one was open for 18% of the time, Pallas kernels for 0%

commit v1 on v0

v1 whole, which is shorter than its diff:
```python
import functools
import math

import jax
import jax.numpy as jnp
from jax import lax
from jax.experimental import pallas as pl
from jax.experimental.pallas import tpu as pltpu
from jax.sharding import PartitionSpec as P

NSEG = 16
MESH = pl.DeviceIdType.MESH
UP, DOWN, ACROSS, SIB = range(4)


def nearest(nz):
    return [sorted(range(nz), key=lambda o: (abs(o - z), o)) for z in range(nz)]


def kernel(ny, nz, tile, a_ref, g_ref, code_ref, e_ref, out_ref, acts, grads, codes, ebuf, acc, red,
           send, recv, own_sem, e_sem, g_send, g_recv, c_send, c_recv, r_send, r_recv):
    n = ny * nz
    rows, tokens = a_ref.shape
    kk = e_ref.shape[0]
    core = lax.axis_index("blk")
    other = 1 - core
    me = lax.axis_index("cols")
    z, y = me // ny, me % ny
    table = nearest(nz)
    order = []
    for i in range(nz):
        pick = jnp.int32(0)
        for zz in range(nz):
            pick = pick + jnp.where(z == zz, jnp.int32(table[zz][i]), jnp.int32(0))
        order.append(pick)

    barrier = pltpu.get_barrier_semaphore()
    for i in range(1, n):
        pl.semaphore_signal(barrier, inc=1, device_id={"cols": lax.rem(me + i, n)}, device_id_type=MESH)
    pl.semaphore_signal(barrier, inc=1, device_id={"blk": other}, device_id_type=MESH)
    pl.semaphore_wait(barrier, n)

    def move(j, kind, first):
        src = a_ref if first else acts.at[j, core]
        dest = {UP: {"cols": me + ny}, DOWN: {"cols": me - ny}, ACROSS: {"cols": z * ny + (1 - y)}, SIB: {"blk": other}}[kind]
        return pltpu.make_async_remote_copy(
            src_ref=src, dst_ref=acts.at[j, core], send_sem=send.at[j, kind], recv_sem=recv.at[j, core],
            device_id=dest, device_id_type=MESH)

    def arrived(j, c):
        pltpu.make_async_remote_copy(
            src_ref=acts.at[j, c], dst_ref=acts.at[j, c], send_sem=send.at[j, SIB], recv_sem=recv.at[j, c],
            device_id={"blk": other}, device_id_type=MESH).wait_recv()

    def load(p, j):
        return pltpu.make_async_copy(e_ref.at[:, pl.ds(pl.multiple_of(j * rows, 16), rows), :], ebuf.at[p % 2], e_sem.at[p % 2])

    def gswap():
        return pltpu.make_async_remote_copy(src_ref=g_ref, dst_ref=grads.at[core], send_sem=g_send, recv_sem=g_recv,
                                            device_id={"blk": other}, device_id_type=MESH)

    def cswap():
        return pltpu.make_async_remote_copy(src_ref=code_ref, dst_ref=codes.at[core], send_sem=c_send, recv_sem=c_recv,
                                            device_id={"blk": other}, device_id_type=MESH)

    own = [pltpu.make_async_copy(a_ref, acts.at[me, core], own_sem.at[0]),
           pltpu.make_async_copy(g_ref, grads.at[core], own_sem.at[1]),
           pltpu.make_async_copy(code_ref, codes.at[core], own_sem.at[2])]

    @pl.when(z < nz - 1)
    def _():
        move(me, UP, True).start()

    @pl.when(z > 0)
    def _():
        move(me, DOWN, True).start()

    if ny > 1:
        move(me, ACROSS, True).start()
    move(me, SIB, True).start()
    for copy in own:
        copy.start()
    gswap().start()
    cswap().start()

    seq = [(0, 0)]
    for i in range(1, nz):
        seq.append((i, 0))
        if ny > 1:
            seq.append((i - 1, 1))
    if ny > 1:
        seq.append((nz - 1, 1))

    def chunk(item):
        i, far = item
        return order[i] * ny + ((1 - y) if far else y)

    load(0, chunk(seq[0])).start()
    acc[...] = jnp.zeros_like(acc)
    for copy in own:
        copy.wait()

    def compute(p, j, c):
        @pl.loop(0, tokens // tile)
        def _(t):
            cols = pl.ds(pl.multiple_of(t * tile, tile), tile)
            g = grads[c, :, cols]
            a = acts[j, c, :, cols].astype(jnp.float32)
            for k in range(kk):
                q = jnp.dot(ebuf[p % 2, k], g, preferred_element_type=jnp.float32)
                acc[k, c, :, cols] += jnp.sum((q * a).reshape(rows // 8, 8, tile), axis=0)

    def hop(h):
        @pl.when(z - h >= 0)
        def _():
            j = me - h * ny
            arrived(j, core)

            @pl.when(z < nz - 1)
            def _():
                move(j, UP, False).start()
            if ny > 1:
                move(j, ACROSS, False).start()
            move(j, SIB, False).start()

        @pl.when(z + h <= nz - 1)
        def _():
            j = me + h * ny
            arrived(j, core)

            @pl.when(z > 0)
            def _():
                move(j, DOWN, False).start()
            if ny > 1:
                move(j, ACROSS, False).start()
            move(j, SIB, False).start()

    for p, item in enumerate(seq):
        i, far = item
        j = chunk(item)
        if i > 0 and not far:
            hop(i)
        if far:
            arrived(j, core)
            move(j, SIB, False).start()
        if p + 1 < n:
            load(p + 1, chunk(seq[p + 1])).start()
        load(p, j).wait()
        compute(p, j, core)
        if p == 0:
            gswap().wait_recv()
        arrived(j, other)
        compute(p, j, other)

    cswap().wait_recv()
    lane = lax.broadcasted_iota(jnp.int32, (8, 128), 1)
    row = lax.broadcasted_iota(jnp.int32, (8, 128), 0)
    part = jnp.zeros((8, 128), jnp.float32)
    for k in range(kk):
        for s in range(NSEG):
            tot = jnp.zeros((8, 128), jnp.float32)
            for c in range(2):
                hit = jnp.where(codes[c] == s, acc[k, c], 0.0)
                for b in range(tokens // 128):
                    tot = tot + hit[:, b * 128:(b + 1) * 128]
            val = jnp.sum(jnp.sum(tot, axis=0, keepdims=True), axis=1, keepdims=True)
            part = part + jnp.where((lane == s) & (row == k), jnp.broadcast_to(val, (8, 128)), 0.0)
    bits = n.bit_length() - 1

    def share(b):
        if b < bits:
            size = 1 << b
            up = (me // size) % 2
            dest = {"cols": me + size - 2 * size * up}
        else:
            dest = {"blk": other}
        return pltpu.make_async_remote_copy(src_ref=red.at[b, 0], dst_ref=red.at[b, 1], send_sem=r_send.at[b],
                                            recv_sem=r_recv.at[b], device_id=dest, device_id_type=MESH)

    for b in range(bits):
        red[b, 0] = part
        share(b).start()
        share(b).wait_recv()
        part = part + red[b, 1]
    red[bits, 0] = part
    share(bits).start()
    share(bits).wait_recv()
    theirs = red[bits, 1]
    out_ref[0] = jnp.where(core == 0, part, theirs)
    out_ref[1] = jnp.where(core == 0, theirs, part)

    for b in range(bits + 1):
        share(b).wait_send()
    gswap().wait_send()
    cswap().wait_send()

    for i in range(nz):
        j = order[i] * ny + y
        first = i == 0

        @pl.when((order[i] <= z) & (z < nz - 1))
        def _():
            move(j, UP, first).wait_send()

        @pl.when((order[i] >= z) & (z > 0))
        def _():
            move(j, DOWN, first).wait_send()
        if ny > 1:
            move(j, ACROSS, first).wait_send()
            move(order[i] * ny + (1 - y), SIB, False).wait_send()
        move(j, SIB, first).wait_send()


def fused(n, at, gt, code, eigvecs):
    ny = 2 if n == 8 else 1
    nz = n // ny
    rows, tokens = at.shape
    width = gt.shape[0]
    kk = eigvecs.shape[0]
    bits = n.bit_length() - 1
    any_spec = pl.BlockSpec(memory_space=pl.ANY)
    dma = pltpu.SemaphoreType.DMA
    return pl.pallas_call(
        functools.partial(kernel, ny, nz, math.gcd(tokens, 512)),
        out_shape=jax.ShapeDtypeStruct((2, 8, 128), jnp.float32),
        in_specs=[any_spec, any_spec, any_spec, any_spec],
        out_specs=pl.BlockSpec(memory_space=pltpu.VMEM),
        scratch_shapes=[
            pltpu.VMEM((n, 2, rows, tokens), jnp.bfloat16),
            pltpu.VMEM((2, width, tokens), jnp.bfloat16),
            pltpu.VMEM((2, 8, tokens), jnp.int32),
            pltpu.VMEM((2, kk, rows, width), jnp.bfloat16),
            pltpu.VMEM((kk, 2, 8, tokens), jnp.float32),
            pltpu.VMEM((bits + 1, 2, 8, 128), jnp.float32),
            dma((n, 4)), dma((n, 2)), dma((3,)), dma((2,)), dma, dma, dma, dma,
            dma((bits + 1,)), dma((bits + 1,)),
        ],
        compiler_params=pltpu.CompilerParams(collective_id=0, has_side_effects=True, vmem_limit_bytes=58 * 1024 * 1024),
        cost_estimate=pl.CostEstimate(flops=2 * n * rows * 2 * tokens * width * kk, bytes_accessed=eigvecs.size * 2, transcendentals=0),
    )(at, gt, code, eigvecs)


def local(n, acts, grads, eigvecs, seg_ids, keep, queries, eigvals):
    kk = eigvecs.shape[0]
    seg_most = acts.shape[0] * 2 // 8
    code = jnp.where(keep == 1, seg_ids, jnp.int32(-1))
    code = jnp.broadcast_to(code[None, :], (8, code.shape[0]))
    out = fused(n, acts.T, grads.T, code, eigvecs)
    sums = out[:, :kk, :NSEG].reshape(2 * kk, NSEG)
    scores = sums * jnp.float32(1.0 / math.sqrt(seg_most))
    weighted = queries / eigvals[None, :]
    influence = jnp.dot(weighted, scores, precision=lax.Precision.HIGHEST)
    return (scores, influence)


def solution(mesh):
    placed = (
        P(("rep", "blk"), "cols"),
        P(("rep", "blk"), "cols"),
        P("blk", None, "cols"),
        P(("rep", "blk")),
        P(("rep", "blk")),
        P("rep", None),
        P(),
    )
    return jax.shard_map(
        functools.partial(local, mesh.shape["cols"]),
        mesh=mesh,
        in_specs=placed,
        out_specs=(P(None, "rep"), P(None, "rep")),
        check_vma=False,
    )
```

time: 229 us -> 115 us (0.50)
  waiting for transfers between devices: 110 us -> 0 us
  Pallas kernels: 0 us -> 105 us
  matrix products: 65.9 us -> 0.88 us
  blocking collectives: 30.4 us -> 0 us
  between operations: 14.1 us -> 0.65 us
    all_gather x1 -> x0, waiting for transfers between devices: 110 us -> none  [local(): features = lax.all_gather(acts, 'cols', axis=1, tiled=True)]
    pallas_call x0 -> x1, Pallas kernels: none -> 105 us  [fused(): pl.pallas_call(functools.partial(kernel, ny, nz, math.gcd(tokens, 512)),...]
    dot_general x4 -> x0, matrix products: 65 us -> none  [the longest x2 64 us: block_scores(): jnp.einsum('td,kdf->ktf', features, weights, preferred_element_type=jnp.f...]
    psum x1 -> x0, blocking collectives: 30.4 us -> none  [local(): sums = lax.psum(total, ('cols', 'blk'))]
    convert_element_type x1 -> x0, local copies, waits for them, and re-layouts: 6.2 us -> none  [block_scores(): terms = jnp.sum(proj * grad_rows.astype(jnp.float32)[None, :, :], axis=2)]
    unnamed x12 -> x7, local copies, waits for them, and re-layouts: 0.03 us -> 5.95 us
  transfers between devices with their start and end apart: 2 -> 0, of which waited for: 1 -> 0; matrix products, arithmetic and copies ran while one was open for 18% -> 0% of each run, Pallas kernels for 0% -> 0%
where the time goes in v1:
time: 115 us; the launch traced here: 114 us
  Pallas kernels  105 us (91%)
  local copies, waits for them, and re-layouts  6.57 us (6%)
  other arithmetic  1.41 us (1%)
    pallas_call x1, Pallas kernels, fused(): pl.pallas_call(functools.partial(kernel, ny, nz, math.gcd(tokens, 512)),...  105 us
    unnamed x7, local copies, waits for them, and re-layouts  5.95 us

profile of v1, /device:TPU:0, one launch (start us, length us, event | category | flops | bytes accessed | tf_op | source)
XLA Modules:
  0.0 114.3 jit_solution(1480064254992758392)
XLA Ops:
  0.6 0.7 compare_select_fusion
  1.3 0.6 broadcast_in_dim.12.code_ref
  2.0 5.9 %copy.9 = bf16[1024,1792]{0,1:T(8,128)(2,1)} copy(bf16[1024,1792]{1,0:T(8,128)(2,1)} %param.8) | data formatting | bytes 7340032 | tf_op args[1]
  7.9 0.0 copy-start.1
  7.9 0.0 copy-start.2
  7.9 104.8 %shard_map.86 = f32[2,8,128]{2,1,0:T(8,128)} custom-call(bf16[448,1024]{1,0:T(8,128)(2,1)} %bitcast.7, bf16[1792,1024]{1,0:T(8,128)(2,1)} %bitcast.4, s32[8,1024]{1,0:T(8,128)} %broadcast_in_dim.12.code_ref, bf16[2,3584,1792]{2,1,0:T(8,128)(2,1)} %e_ref.1), custom_call_target="tpu_custom_call" | custom-call | flops 52613349376 | bytes 25690112 | tf_op jit(solution)/shard_map/pallas_call | solution.py:223
  112.7 0.7 slice_multiply_fusion
  113.4 0.0 copy-start
  113.4 0.0 copy-done.1
  113.4 0.0 copy-done.2
  113.4 0.9 fusion
  114.3 0.0 copy-done
Async XLA Ops:
  7.9 105.5 %copy-start.1 = (f32[16,4]{0,1:T(4,128)S(1)}, f32[16,4]{0,1:T(4,128)}, u32[]{:S(2)}) copy-start(f32[16,4]{0,1:T(4,128)} %param.12) | copy-start | bytes 772
  7.9 105.5 %copy-start.2 = (f32[4]{0:T(128)S(1)}, f32[4]{0:T(128)}, u32[]{:S(2)}) copy-start(f32[4]{0:T(128)} %param.13) | copy-start | bytes 52
  113.4 0.9 copy-start

commit v2 on v1

--- a/solution.py
+++ b/solution.py
@@ -17,11 +17,13 @@
     return [sorted(range(nz), key=lambda o: (abs(o - z), o)) for z in range(nz)]
 
 
-def kernel(ny, nz, tile, a_ref, g_ref, code_ref, e_ref, out_ref, acts, grads, codes, ebuf, acc, red,
-           send, recv, own_sem, e_sem, g_send, g_recv, c_send, c_recv, r_send, r_recv):
+def kernel(ny, nz, tile, scale, a_ref, g_ref, e_ref, seg_ref, keep_ref, q_ref, v_ref, scores_ref, inf_ref, acts, grads, codes, ebuf, acc, red,
+           send, recv, small_send, small_recv, own_sem, e_sem, g_send, g_recv, c_send, c_recv, r_send, r_recv):
     n = ny * nz
     rows, tokens = a_ref.shape
     kk = e_ref.shape[0]
+    small = 128 if ny > 1 else 0
+    large = tokens - small
     core = lax.axis_index("blk")
     other = 1 - core
     me = lax.axis_index("cols")
@@ -40,16 +42,23 @@
     pl.semaphore_signal(barrier, inc=1, device_id={"blk": other}, device_id_type=MESH)
     pl.semaphore_wait(barrier, n)
 
-    def move(j, kind, first):
-        src = a_ref if first else acts.at[j, core]
+    spans = (pl.ds(0, large), pl.ds(large, small))
+    sends, recvs = (send, small_send), (recv, small_recv)
+
+    def move(j, kind, first, piece=0):
+        if first:
+            src = a_ref.at[:, spans[piece]]
+        else:
+            src = acts.at[j, core, :, spans[piece]]
         dest = {UP: {"cols": me + ny}, DOWN: {"cols": me - ny}, ACROSS: {"cols": z * ny + (1 - y)}, SIB: {"blk": other}}[kind]
         return pltpu.make_async_remote_copy(
-            src_ref=src, dst_ref=acts.at[j, core], send_sem=send.at[j, kind], recv_sem=recv.at[j, core],
-            device_id=dest, device_id_type=MESH)
-
-    def arrived(j, c):
+            src_ref=src, dst_ref=acts.at[j, core, :, spans[piece]], send_sem=sends[piece].at[j, kind],
+            recv_sem=recvs[piece].at[j, core], device_id=dest, device_id_type=MESH)
+
+    def arrived(j, c, piece=0):
+        ref = acts.at[j, c, :, spans[piece]]
         pltpu.make_async_remote_copy(
-            src_ref=acts.at[j, c], dst_ref=acts.at[j, c], send_sem=send.at[j, SIB], recv_sem=recv.at[j, c],
+            src_ref=ref, dst_ref=ref, send_sem=sends[piece].at[j, SIB], recv_sem=recvs[piece].at[j, c],
             device_id={"blk": other}, device_id_type=MESH).wait_recv()
 
     def load(p, j):
@@ -60,12 +69,14 @@
                                             device_id={"blk": other}, device_id_type=MESH)
 
     def cswap():
-        return pltpu.make_async_remote_copy(src_ref=code_ref, dst_ref=codes.at[core], send_sem=c_send, recv_sem=c_recv,
+        return pltpu.make_async_remote_copy(src_ref=codes.at[core], dst_ref=codes.at[core], send_sem=c_send, recv_sem=c_recv,
                                             device_id={"blk": other}, device_id_type=MESH)
 
     own = [pltpu.make_async_copy(a_ref, acts.at[me, core], own_sem.at[0]),
-           pltpu.make_async_copy(g_ref, grads.at[core], own_sem.at[1]),
-           pltpu.make_async_copy(code_ref, codes.at[core], own_sem.at[2])]
+           pltpu.make_async_copy(g_ref, grads.at[core], own_sem.at[1])]
+
+    if small:
+        move(me, ACROSS, True, 1).start()
 
     @pl.when(z < nz - 1)
     def _():
@@ -77,10 +88,21 @@
 
     if ny > 1:
         move(me, ACROSS, True).start()
+    if small:
+        @pl.when(z < nz - 1)
+        def _():
+            move(me, UP, True, 1).start()
+
+        @pl.when(z > 0)
+        def _():
+            move(me, DOWN, True, 1).start()
+
+        move(me, SIB, True, 1).start()
     move(me, SIB, True).start()
     for copy in own:
         copy.start()
     gswap().start()
+    codes[core] = jnp.where(keep_ref[...] == 1, seg_ref[...], jnp.int32(-1))
     cswap().start()
 
     seq = [(0, 0)]
@@ -104,10 +126,10 @@
         @pl.loop(0, tokens // tile)
         def _(t):
             cols = pl.ds(pl.multiple_of(t * tile, tile), tile)
-            g = grads[c, :, cols]
+            g = grads[c, cols, :]
             a = acts[j, c, :, cols].astype(jnp.float32)
             for k in range(kk):
-                q = jnp.dot(ebuf[p % 2, k], g, preferred_element_type=jnp.float32)
+                q = lax.dot_general(ebuf[p % 2, k], g, (((1,), (1,)), ((), ())), preferred_element_type=jnp.float32)
                 acc[k, c, :, cols] += jnp.sum((q * a).reshape(rows // 8, 8, tile), axis=0)
 
     def hop(h):
@@ -134,12 +156,37 @@
             if ny > 1:
                 move(j, ACROSS, False).start()
             move(j, SIB, False).start()
+
+    def small_pass(j, up, down):
+        arrived(j, core, 1)
+        if up:
+            @pl.when(z < nz - 1)
+            def _():
+                move(j, UP, False, 1).start()
+        if down:
+            @pl.when(z > 0)
+            def _():
+                move(j, DOWN, False, 1).start()
+        move(j, SIB, False, 1).start()
+
+    def small_hop(h, far):
+        shift = (1 - 2 * y) if far else 0
+
+        @pl.when(z - h >= 0)
+        def _():
+            small_pass(me - h * ny + shift, True, False)
+
+        @pl.when(z + h <= nz - 1)
+        def _():
+            small_pass(me + h * ny + shift, False, True)
 
     for p, item in enumerate(seq):
         i, far = item
         j = chunk(item)
         if i > 0 and not far:
             hop(i)
+            if small:
+                small_hop(i, False)
         if far:
             arrived(j, core)
             move(j, SIB, False).start()
@@ -148,8 +195,14 @@
         load(p, j).wait()
         compute(p, j, core)
         if p == 0:
+            if small:
+                small_pass(z * ny + (1 - y), True, True)
             gswap().wait_recv()
+        elif small and not far:
+            small_hop(i, True)
         arrived(j, other)
+        if small:
+            arrived(j, other, 1)
         compute(p, j, other)
 
     cswap().wait_recv()
@@ -160,9 +213,8 @@
         for s in range(NSEG):
             tot = jnp.zeros((8, 128), jnp.float32)
             for c in range(2):
-                hit = jnp.where(codes[c] == s, acc[k, c], 0.0)
                 for b in range(tokens // 128):
-                    tot = tot + hit[:, b * 128:(b + 1) * 128]
+                    tot = tot + jnp.where(codes[c, b:b + 1, :] == s, acc[k, c, :, b * 128:(b + 1) * 128], 0.0)
             val = jnp.sum(jnp.sum(tot, axis=0, keepdims=True), axis=1, keepdims=True)
             part = part + jnp.where((lane == s) & (row == k), jnp.broadcast_to(val, (8, 128)), 0.0)
     bits = n.bit_length() - 1
@@ -186,8 +238,15 @@
     share(bits).start()
     share(bits).wait_recv()
     theirs = red[bits, 1]
-    out_ref[0] = jnp.where(core == 0, part, theirs)
-    out_ref[1] = jnp.where(core == 0, theirs, part)
+    halves = (jnp.where(core == 0, part, theirs), jnp.where(core == 0, theirs, part))
+    weighted = q_ref[...] / v_ref[...]
+    total = jnp.zeros(inf_ref.shape, jnp.float32)
+    for c in range(2):
+        for k in range(kk):
+            line = halves[c][k:k + 1, :NSEG] * scale
+            scores_ref[c * kk + k:c * kk + k + 1, :] = line
+            total = total + weighted[:, c * kk + k:c * kk + k + 1] * line
+    inf_ref[...] = total
 
     for b in range(bits + 1):
         share(b).wait_send()
@@ -209,48 +268,54 @@
             move(j, ACROSS, first).wait_send()
             move(order[i] * ny + (1 - y), SIB, False).wait_send()
         move(j, SIB, first).wait_send()
-
-
-def fused(n, at, gt, code, eigvecs):
+        if small:
+            f = order[i] * ny + (1 - y)
+
+            @pl.when((order[i] <= z) & (z < nz - 1))
+            def _():
+                move(j, UP, first, 1).wait_send()
+                move(f, UP, False, 1).wait_send()
+
+            @pl.when((order[i] >= z) & (z > 0))
+            def _():
+                move(j, DOWN, first, 1).wait_send()
+                move(f, DOWN, False, 1).wait_send()
+            if first:
+                move(j, ACROSS, first, 1).wait_send()
+            move(j, SIB, first, 1).wait_send()
+            move(f, SIB, False, 1).wait_send()
+
+
+def local(n, acts, grads, eigvecs, seg_ids, keep, queries, eigvals):
     ny = 2 if n == 8 else 1
     nz = n // ny
-    rows, tokens = at.shape
-    width = gt.shape[0]
+    tokens, rows = acts.shape
+    width = grads.shape[1]
     kk = eigvecs.shape[0]
     bits = n.bit_length() - 1
     any_spec = pl.BlockSpec(memory_space=pl.ANY)
+    vmem = pl.BlockSpec(memory_space=pltpu.VMEM)
     dma = pltpu.SemaphoreType.DMA
+    scale = 1.0 / math.sqrt(tokens * 2 // 8)
     return pl.pallas_call(
-        functools.partial(kernel, ny, nz, math.gcd(tokens, 512)),
-        out_shape=jax.ShapeDtypeStruct((2, 8, 128), jnp.float32),
-        in_specs=[any_spec, any_spec, any_spec, any_spec],
-        out_specs=pl.BlockSpec(memory_space=pltpu.VMEM),
+        functools.partial(kernel, ny, nz, math.gcd(tokens, 512), scale),
+        out_shape=(jax.ShapeDtypeStruct((2 * kk, NSEG), jnp.float32),
+                   jax.ShapeDtypeStruct((queries.shape[0], NSEG), jnp.float32)),
+        in_specs=[any_spec] * 3 + [vmem] * 4,
+        out_specs=(vmem, vmem),
         scratch_shapes=[
             pltpu.VMEM((n, 2, rows, tokens), jnp.bfloat16),
-            pltpu.VMEM((2, width, tokens), jnp.bfloat16),
-            pltpu.VMEM((2, 8, tokens), jnp.int32),
+            pltpu.VMEM((2, tokens, width), jnp.bfloat16),
+            pltpu.VMEM((2, tokens // 128, 128), jnp.int32),
             pltpu.VMEM((2, kk, rows, width), jnp.bfloat16),
             pltpu.VMEM((kk, 2, 8, tokens), jnp.float32),
             pltpu.VMEM((bits + 1, 2, 8, 128), jnp.float32),
-            dma((n, 4)), dma((n, 2)), dma((3,)), dma((2,)), dma, dma, dma, dma,
+            dma((n, 4)), dma((n, 2)), dma((n, 4)), dma((n, 2)), dma((2,)), dma((2,)), dma, dma, dma, dma,
             dma((bits + 1,)), dma((bits + 1,)),
         ],
         compiler_params=pltpu.CompilerParams(collective_id=0, has_side_effects=True, vmem_limit_bytes=58 * 1024 * 1024),
         cost_estimate=pl.CostEstimate(flops=2 * n * rows * 2 * tokens * width * kk, bytes_accessed=eigvecs.size * 2, transcendentals=0),
-    )(at, gt, code, eigvecs)
-
-
-def local(n, acts, grads, eigvecs, seg_ids, keep, queries, eigvals):
-    kk = eigvecs.shape[0]
-    seg_most = acts.shape[0] * 2 // 8
-    code = jnp.where(keep == 1, seg_ids, jnp.int32(-1))
-    code = jnp.broadcast_to(code[None, :], (8, code.shape[0]))
-    out = fused(n, acts.T, grads.T, code, eigvecs)
-    sums = out[:, :kk, :NSEG].reshape(2 * kk, NSEG)
-    scores = sums * jnp.float32(1.0 / math.sqrt(seg_most))
-    weighted = queries / eigvals[None, :]
-    influence = jnp.dot(weighted, scores, precision=lax.Precision.HIGHEST)
-    return (scores, influence)
+    )(acts.T, grads, eigvecs, seg_ids.reshape(-1, 128), keep.reshape(-1, 128), queries, eigvals[None, :])
 
 
 def solution(mesh):

time: 115 us -> 111 us (0.965)
  local copies, waits for them, and re-layouts: 6.57 us -> 3.88 us
  other arithmetic: 1.41 us -> 0 us
    unnamed x7 -> x3, local copies, waits for them, and re-layouts: 5.95 us -> 3.88 us
where the time goes in v2:
time: 111 us; the launch traced here: 110 us
  Pallas kernels  106 us (95%)
  local copies, waits for them, and re-layouts  3.88 us (3%)
    pallas_call x1, Pallas kernels, local(): pl.pallas_call(functools.partial(kernel, ny, nz, math.gcd(tokens, 512), s...  106 us
    unnamed x3, local copies, waits for them, and re-layouts  3.88 us

profile of v2, /device:TPU:0, one launch (start us, length us, event | category | flops | bytes accessed | tf_op | source)
XLA Modules:
  0.0 110.2 jit_solution(13261301215623888974)
XLA Ops:
  0.6 1.4 %copy.9.q_ref = f32[16,4]{1,0:T(8,128)} copy(f32[16,4]{0,1:T(4,128)} %param.12) | data formatting | bytes 512 | tf_op args[5]
  2.0 105.7 %shard_map.86 = (f32[4,16]{1,0:T(4,128)}, f32[16,16]{1,0:T(8,128)}) custom-call(bf16[448,1024]{1,0:T(8,128)(2,1)} %bitcast.4, bf16[1024,1792]{1,0:T(8,128)(2,1)} %g_ref.1, bf16[2,3584,1792]{2,1,0:T(8,128)(2,1)} %e_ref.1, s32[8,128]{1,0:T(8,128)} %bitcast.5, s32[8,128]{1,0:T(8,128)} %bitcast.6, f32[16,4]{1,0:T(8,128)} %copy.9.q_ref, f32[1,4]{1,0:T(1,128)} %bitcast.7), custom_call_target="tpu_custom_call" | custom-call | flops 52613349376 | bytes 25690112 | tf_op jit(solution)/shard_map/pallas_call | solution.py:300
  107.7 1.2 %copy.12 = f32[4,16]{1,0:T(4,128)} copy(f32[4,16]{1,0:T(4,128)} %get-tuple-element.4) | data formatting | bytes 512
  108.9 1.3 %copy.13 = f32[16,16]{1,0:T(8,128)} copy(f32[16,16]{1,0:T(8,128)} %get-tuple-element.5) | data formatting | bytes 2048
